TPU v7x, 32 devices: a whole 2x2x4 slice. The times are simulated.
32 devices in a mesh: dp: 4 (over y, x), tensor: 4 (over z), section: 2 (over core).
Axes of the slice: x: 2, y: 2, z: 4, core: 2. Of those that a mesh axis runs over, the one named last changes fastest.
Arguments:
- tokens: bfloat16 [8, 2, 512, 768], P('dp', None, 'tensor'), may hold values from -6 to 6
- cotangent: bfloat16 [8, 2, 512, 768], P('dp', None, 'tensor'), may hold values from -6 to 6
- document_starts: int32 [8, 2, 4], P('dp'), may hold values from 0 to 511, as said below
- valid_count: int32 [8, 2], P('dp'), may hold values from 448 to 512
- reset_flags: int32 [8, 1], P('dp'), may hold values 0 or 1
- memory_init: float32 [16, 768], P('tensor', ('dp', 'section')), may hold values from -6 to 6
- attention_in: float32 [2, 768, 3, 768], P('section', 'dp', None, 'tensor'), may hold values from -0.21875 to 0.21875
- attention_out: float32 [2, 768, 768], P('section', 'tensor', 'dp'), may hold values from -2.5 to 2.5
- feed_expand: float32 [2, 768, 3072], P('section', 'dp', 'tensor'), may hold values from -0.21875 to 0.21875
- feed_reduce: float32 [2, 3072, 768], P('section', 'tensor', 'dp'), may hold values from -0.109375 to 0.109375
- norm_gains: float32 [2, 2, 768], P('section', None, 'dp'), may hold values from 0.4 to 1.6
- norm_shifts: float32 [2, 2, 768], P('section', None, 'dp'), may hold values from -1.8 to 1.8
Outputs:
- layer_ends: bfloat16 [2, 8, 2, 512, 768], P('section', 'dp', None, 'tensor')
- memory_grad: float32 [16, 768], P('tensor', ('dp', 'section'))
- attention_in_grad: float32 [2, 768, 3, 768], P('section', 'dp', None, 'tensor')
- attention_out_grad: float32 [2, 768, 768], P('section', 'tensor', 'dp')
- feed_expand_grad: float32 [2, 768, 3072], P('section', 'dp', 'tensor')
- feed_reduce_grad: float32 [2, 3072, 768], P('section', 'tensor', 'dp')
- norm_gains_grad: float32 [2, 2, 768], P('section', None, 'dp')
- norm_shifts_grad: float32 [2, 2, 768], P('section', None, 'dp')
Inputs may be any that keep to these rules, and one draw needn't show every extreme that they name: `document_starts`: each segment's 4 starts increase strictly; the first is 0 and all lie below 512; a document runs from its start to the next start, the last to the segment's end.
All inputs are finite; a program needn't handle non-finite values. No bound on the sum of `reset_flags` on one device may be relied on, other than what follows from the above.
Results may differ from a plain program's by a relative error of at most 0.04.
Values may be sent and summed in bfloat16 or wider, within the bound.
No kernel may reach another device: no remote copies, remote signals or barrier semaphores. Data moves between devices by JAX's collectives and lax.ppermute only.
A program may use at most 192 MiB of HBM per device.

v0:
```python
import jax
import jax.numpy as jnp
from jax import lax
from jax.sharding import PartitionSpec as P

HEAD = 64


def shifted(block, axis, distance):
    devices = range(lax.axis_size(axis))
    route = [(i - distance, i) for i in devices if i - distance in devices]
    return lax.ppermute(block, axis, route)


def norm_rows(values, gain_row, shift_row):
    mean_row = jnp.mean(values, -1, keepdims=True)
    centred = values - mean_row
    spread = jnp.mean(centred * centred, -1, keepdims=True)
    return centred * lax.rsqrt(spread + 1e-05) * gain_row + shift_row


def gelu_exact(values):
    return 0.5 * values * (1.0 + lax.erf(values * 0.7071067811865476))


def gather_rows(values):
    return lax.all_gather(values, "tensor", axis=0, tiled=True)


def reduce_rows(left_side, right_side, einsum_form):
    return lax.psum_scatter(
        jnp.einsum(einsum_form, left_side, right_side, preferred_element_type=jnp.float32).astype(
            jnp.bfloat16
        ),
        "tensor",
        scatter_dimension=0,
        tiled=True,
    ).astype(jnp.float32)


def send_down(values):
    return shifted(values, "section", 1)


def send_up(values):
    return shifted(values, "section", -1)


def allowed_rows(starts, valid, tensor_count, memory_dev, segment_dev):
    row_dev = memory_dev + segment_dev
    row_place = jnp.arange(tensor_count * row_dev)
    row_inner = row_place % row_dev
    is_memory = row_inner < memory_dev
    token_index = row_place // row_dev * segment_dev + row_inner - memory_dev
    doc_index = jnp.sum((starts[:, None, :] <= token_index[None, :, None]).astype(jnp.int32), -1)
    key_live = is_memory[None, :] | (token_index[None, :] < valid[:, None])
    same_doc = doc_index[:, :, None] == doc_index[:, None, :]
    either_memory = is_memory[:, None] | is_memory[None, :]
    return key_live[:, None, :] & (either_memory[None] | same_doc)


def attention_scores(projected, allowed, heads_local):
    row_total, batch_size = (projected.shape[0], projected.shape[1])
    split_qkv = projected.reshape(row_total, batch_size, 3, heads_local, HEAD)
    queries = split_qkv[:, :, 0]
    key_rows = split_qkv[:, :, 1]
    value_rows = split_qkv[:, :, 2]
    scores = jnp.einsum(
        "qbhe,kbhe->bhqk", queries, key_rows, preferred_element_type=jnp.float32
    ) * HEAD ** (-0.5)
    scores = jnp.where(allowed[:, None], scores, -1000000000.0)
    return (queries, key_rows, value_rows, scores)


def layer_forward(row_block, allowed, weights, heads_local):
    inputs_weight, outputs_weight, expand_weight, reduce_weight, gain_rows, shift_rows = weights
    gains = gain_rows.astype(jnp.float32)
    shifts = shift_rows.astype(jnp.float32)
    gathered = gather_rows(row_block.astype(jnp.bfloat16))
    row_total, batch_size = (gathered.shape[0], gathered.shape[1])
    projected = jnp.einsum(
        "rbd,dkc->rbkc", gathered, inputs_weight, preferred_element_type=jnp.float32
    ).astype(jnp.bfloat16)
    queries, key_rows, value_rows, scores = attention_scores(projected, allowed, heads_local)
    top_score = jnp.max(scores, -1, keepdims=True)
    exp_scores = jnp.exp(scores - top_score)
    total_mass = jnp.sum(exp_scores, -1, keepdims=True)
    log_mass = top_score + jnp.log(total_mass)
    probs_low = (exp_scores / total_mass).astype(jnp.bfloat16)
    mixed = jnp.einsum(
        "bhqk,kbhe->qbhe", probs_low, value_rows, preferred_element_type=jnp.float32
    ).astype(jnp.bfloat16)
    mixed = mixed.reshape(row_total, batch_size, heads_local * HEAD)
    attn_sum = reduce_rows(mixed, outputs_weight, "rbc,cd->rbd")
    first_sum = row_block + attn_sum
    normed = norm_rows(first_sum, gains[0], shifts[0])
    normed_all = gather_rows(normed.astype(jnp.bfloat16))
    hidden = jnp.einsum(
        "rbd,df->rbf", normed_all, expand_weight, preferred_element_type=jnp.float32
    )
    active = gelu_exact(hidden).astype(jnp.bfloat16)
    ffn_sum = reduce_rows(active, reduce_weight, "rbf,fd->rbd")
    second_sum = normed + ffn_sum
    result = norm_rows(second_sum, gains[1], shifts[1]).astype(jnp.bfloat16)
    kept_state = (
        gathered,
        projected,
        log_mass,
        mixed,
        first_sum,
        normed,
        normed_all,
        hidden,
        active,
        second_sum,
    )
    return (result, kept_state)


def layer_backward(grad_out, kept_state, allowed, weights, heads_local):
    inputs_weight, outputs_weight, expand_weight, reduce_weight, gain_rows, shift_rows = weights
    (
        gathered,
        projected,
        log_mass,
        mixed,
        first_sum,
        normed,
        normed_all,
        hidden,
        active,
        second_sum,
    ) = kept_state
    gains = gain_rows.astype(jnp.float32)
    shifts = shift_rows.astype(jnp.float32)
    row_total, batch_size = (gathered.shape[0], gathered.shape[1])
    second_value, second_pull = jax.vjp(norm_rows, second_sum, gains[1], shifts[1])
    grad_second, gain_two, shift_two = second_pull(grad_out)
    ffn_grad_all = gather_rows(grad_second.astype(jnp.bfloat16))
    grad_active = jnp.einsum(
        "rbd,fd->rbf", ffn_grad_all, reduce_weight, preferred_element_type=jnp.float32
    )
    reduce_grad = jnp.einsum(
        "rbf,rbd->fd", active, ffn_grad_all, preferred_element_type=jnp.float32
    )
    gelu_value, gelu_pull = jax.vjp(gelu_exact, hidden)
    grad_hidden = gelu_pull(grad_active)[0].astype(jnp.bfloat16)
    expand_grad = jnp.einsum(
        "rbd,rbf->df", normed_all, grad_hidden, preferred_element_type=jnp.float32
    )
    grad_normed = grad_second + reduce_rows(grad_hidden, expand_weight, "rbf,df->rbd")
    first_value, first_pull = jax.vjp(norm_rows, first_sum, gains[0], shifts[0])
    grad_first, gain_one, shift_one = first_pull(grad_normed)
    attn_grad_all = gather_rows(grad_first.astype(jnp.bfloat16))
    grad_mixed = jnp.einsum(
        "rbd,cd->rbc", attn_grad_all, outputs_weight, preferred_element_type=jnp.float32
    ).astype(jnp.bfloat16)
    outputs_grad = jnp.einsum(
        "rbc,rbd->cd", mixed, attn_grad_all, preferred_element_type=jnp.float32
    )
    queries, key_rows, value_rows, scores = attention_scores(projected, allowed, heads_local)
    probs = jnp.exp(scores - log_mass)
    probs_low = probs.astype(jnp.bfloat16)
    grad_heads = grad_mixed.reshape(row_total, batch_size, heads_local, HEAD)
    grad_probs = jnp.einsum(
        "qbhe,kbhe->bhqk", grad_heads, value_rows, preferred_element_type=jnp.float32
    )
    grad_scores = (probs * (grad_probs - jnp.sum(probs * grad_probs, -1, keepdims=True))).astype(
        jnp.bfloat16
    )
    scale = HEAD ** (-0.5)
    grad_queries = (
        jnp.einsum("bhqk,kbhe->qbhe", grad_scores, key_rows, preferred_element_type=jnp.float32)
        * scale
    ).astype(jnp.bfloat16)
    grad_keys = (
        jnp.einsum("bhqk,qbhe->kbhe", grad_scores, queries, preferred_element_type=jnp.float32)
        * scale
    ).astype(jnp.bfloat16)
    grad_values = jnp.einsum(
        "bhqk,qbhe->kbhe", probs_low, grad_heads, preferred_element_type=jnp.float32
    ).astype(jnp.bfloat16)
    grad_projected = jnp.stack([grad_queries, grad_keys, grad_values], 2).reshape(
        row_total, batch_size, 3, heads_local * HEAD
    )
    inputs_grad = jnp.einsum(
        "rbd,rbkc->dkc", gathered, grad_projected, preferred_element_type=jnp.float32
    )
    grad_rows = grad_first + reduce_rows(grad_projected, inputs_weight, "rbkc,dkc->rbd")
    gain_grads = jnp.stack([gain_one, gain_two], 0)
    shift_grads = jnp.stack([shift_one, shift_two], 0)
    return (
        grad_rows,
        (inputs_grad, outputs_grad, expand_grad, reduce_grad, gain_grads, shift_grads),
    )


def shards(
    tokens,
    cotangent,
    document_starts,
    valid_count,
    reset_flags,
    memory_init,
    attention_in,
    attention_out,
    feed_expand,
    feed_reduce,
    norm_gains,
    norm_shifts,
):
    tensor_count = lax.axis_size("tensor")
    tensor_place = lax.axis_index("tensor")
    is_first = lax.axis_index("section") == 0
    seq_local, segments, segment_dev, width = tokens.shape
    half_count = seq_local // 2
    memory_dev = memory_init.shape[0]
    row_dev = memory_dev + segment_dev
    heads_local = attention_in.shape[3] // HEAD
    item_total = 2 * segments
    memory_rows = lax.all_gather(
        memory_init.astype(jnp.bfloat16), ("dp", "section"), axis=1, tiled=True
    )
    init_rows = memory_rows[:, None, :]
    gathered_weights = (
        lax.all_gather(attention_in.astype(jnp.bfloat16), "dp", axis=1, tiled=True),
        lax.all_gather(attention_out.astype(jnp.bfloat16), "dp", axis=2, tiled=True),
        lax.all_gather(feed_expand.astype(jnp.bfloat16), "dp", axis=1, tiled=True),
        lax.all_gather(feed_reduce.astype(jnp.bfloat16), "dp", axis=2, tiled=True),
        lax.all_gather(norm_gains.astype(jnp.bfloat16), "dp", axis=2, tiled=True),
        lax.all_gather(norm_shifts.astype(jnp.bfloat16), "dp", axis=2, tiled=True),
    )
    weights = tuple((piece_part[0] for piece_part in gathered_weights))

    def item_mask(item_index):
        half_index, segment = (item_index % 2, item_index // 2)
        starts = document_starts[half_index * half_count : (half_index + 1) * half_count, segment]
        valid = valid_count[half_index * half_count : (half_index + 1) * half_count, segment]
        return allowed_rows(starts, valid, tensor_count, memory_dev, segment_dev)

    mask_list = [item_mask(item_index) for item_index in range(item_total)]
    from_before = jnp.zeros((row_dev, half_count, width), jnp.bfloat16)
    memory_back = jnp.zeros((memory_dev, half_count, width), jnp.bfloat16)
    saved = []
    outputs = [None] * item_total
    for step_index in range(item_total + 1):
        item_one = min(step_index, item_total - 1)
        item_two = max(step_index - 1, 0)
        half_index, segment = (item_one % 2, item_one // 2)
        seq_lo, seq_hi = (half_index * half_count, (half_index + 1) * half_count)
        if segment == 0:
            memory_in = init_rows
        else:
            reset_now = reset_flags[seq_lo:seq_hi, segment - 1] > 0
            memory_in = jnp.where(reset_now[None, :, None], init_rows, memory_back)
        token_rows = jnp.swapaxes(tokens[seq_lo:seq_hi, segment], 0, 1)
        first_rows = jnp.concatenate([memory_in, token_rows], 0)
        row_block = jnp.where(is_first, first_rows, from_before).astype(jnp.float32)
        allowed = jnp.where(is_first, mask_list[item_one], mask_list[item_two])
        result, kept_state = layer_forward(row_block, allowed, weights, heads_local)
        saved.append((kept_state, allowed))
        from_before = send_down(result)
        memory_back = send_up(result[:memory_dev])
        if step_index >= 1:
            outputs[step_index - 1] = result[memory_dev:]
    token_local = tensor_place * segment_dev + jnp.arange(segment_dev)
    grad_sums = tuple((jnp.zeros(weight_part.shape, jnp.float32) for weight_part in weights))
    memory_sum = jnp.zeros((memory_dev, width), jnp.float32)
    d_from_after = jnp.zeros((row_dev, half_count, width), jnp.bfloat16)
    d_memory = jnp.zeros((memory_dev, half_count, width), jnp.bfloat16)
    token_grads = [None] * item_total
    for back_index in range(item_total + 1):
        kept_state, allowed = saved[item_total - back_index]
        item_two = max(item_total - 1 - back_index, 0)
        item_one = min(item_total - back_index, item_total - 1)
        half_two, segment_two = (item_two % 2, item_two // 2)
        lo_two, hi_two = (half_two * half_count, (half_two + 1) * half_count)
        live_tokens = token_local[:, None] < valid_count[lo_two:hi_two, segment_two][None, :]
        token_cot = jnp.swapaxes(cotangent[lo_two:hi_two, segment_two], 0, 1).astype(jnp.float32)
        token_cot = jnp.where(live_tokens[:, :, None], token_cot, 0.0)
        if segment_two + 1 < segments:
            keep_memory = reset_flags[lo_two:hi_two, segment_two] == 0
            memory_cot = jnp.where(keep_memory[None, :, None], d_memory.astype(jnp.float32), 0.0)
        else:
            memory_cot = jnp.zeros((memory_dev, half_count, width), jnp.float32)
        second_grad = jnp.concatenate([memory_cot, token_cot], 0)
        if back_index >= item_total:
            second_grad = jnp.zeros_like(second_grad)
        if back_index >= 1:
            first_grad = d_from_after.astype(jnp.float32)
        else:
            first_grad = jnp.zeros((row_dev, half_count, width), jnp.float32)
        grad_out = jnp.where(is_first, first_grad, second_grad)
        grad_rows, layer_grads = layer_backward(grad_out, kept_state, allowed, weights, heads_local)
        grad_sums = tuple(
            (total_part + new_part for total_part, new_part in zip(grad_sums, layer_grads))
        )
        grad_low = grad_rows.astype(jnp.bfloat16)
        if back_index >= 1:
            half_one, segment_one = (item_one % 2, item_one // 2)
            lo_one, hi_one = (half_one * half_count, (half_one + 1) * half_count)
            memory_part = grad_low[:memory_dev].astype(jnp.float32)
            if segment_one == 0:
                to_init = jnp.ones((half_count,), bool)
            else:
                to_init = reset_flags[lo_one:hi_one, segment_one - 1] > 0
            routed = jnp.sum(jnp.where(to_init[None, :, None], memory_part, 0.0), 1)
            memory_sum = memory_sum + jnp.where(is_first, routed, 0.0)
            token_grads[item_one] = grad_low[memory_dev:]
        d_memory = send_down(grad_low[:memory_dev])
        d_from_after = send_up(grad_low)
    segment_blocks = []
    for segment in range(segments):
        per_half = []
        for half_index in range(2):
            item_index = 2 * segment + half_index
            chosen = jnp.where(is_first, token_grads[item_index], outputs[item_index])
            per_half.append(jnp.swapaxes(chosen, 0, 1))
        segment_blocks.append(jnp.concatenate(per_half, 0))
    layer_ends = jnp.stack(segment_blocks, 1)[None]
    gain_total, shift_total = lax.psum((grad_sums[4], grad_sums[5]), "tensor")
    reduced = (
        lax.psum_scatter(
            grad_sums[0][None].astype(jnp.bfloat16), "dp", scatter_dimension=1, tiled=True
        ).astype(jnp.float32),
        lax.psum_scatter(
            grad_sums[1][None].astype(jnp.bfloat16), "dp", scatter_dimension=2, tiled=True
        ).astype(jnp.float32),
        lax.psum_scatter(
            grad_sums[2][None].astype(jnp.bfloat16), "dp", scatter_dimension=1, tiled=True
        ).astype(jnp.float32),
        lax.psum_scatter(
            grad_sums[3][None].astype(jnp.bfloat16), "dp", scatter_dimension=2, tiled=True
        ).astype(jnp.float32),
        lax.psum_scatter(
            gain_total[None].astype(jnp.bfloat16), "dp", scatter_dimension=2, tiled=True
        ).astype(jnp.float32),
        lax.psum_scatter(
            shift_total[None].astype(jnp.bfloat16), "dp", scatter_dimension=2, tiled=True
        ).astype(jnp.float32),
    )
    memory_grad = lax.psum_scatter(memory_sum, ("dp", "section"), scatter_dimension=1, tiled=True)
    return (
        layer_ends,
        memory_grad,
        reduced[0],
        reduced[1],
        reduced[2],
        reduced[3],
        reduced[4],
        reduced[5],
    )


def solution(mesh):
    in_specs = (
        P("dp", None, "tensor", None),
        P("dp", None, "tensor", None),
        P("dp", None, None),
        P("dp", None),
        P("dp", None),
        P("tensor", ("dp", "section")),
        P("section", "dp", None, "tensor"),
        P("section", "tensor", "dp"),
        P("section", "dp", "tensor"),
        P("section", "tensor", "dp"),
        P("section", None, "dp"),
        P("section", None, "dp"),
    )
    out_specs = (
        P("section", "dp", None, "tensor", None),
        P("tensor", ("dp", "section")),
        P("section", "dp", None, "tensor"),
        P("section", "tensor", "dp"),
        P("section", "dp", "tensor"),
        P("section", "tensor", "dp"),
        P("section", None, "dp"),
        P("section", None, "dp"),
    )
    return jax.shard_map(shards, mesh=mesh, in_specs=in_specs, out_specs=out_specs, check_vma=False)
```

profile of v0, /device:TPU:0, one launch (start us, length us, event | category | flops | bytes accessed | tf_op | source)
XLA Modules:
  0.0 1589.8 jit_solution(5983131650415631001)
XLA Ops:
  62.4 29.3 %all_gather.83 = bf16[528,1,768]{2,1,0:T(2,128)(2,1)S(1)} all-gather(bf16[132,1,768]{2,1,0:T(2,128)(2,1)S(1)} %copy.212), channel_id=1, replica_groups=mesh['dp'=4,'tensor'=4,'section'=2] {'tensor'}, dimensions={0}, use_global_device_ids=true | all-gather | bytes 1013760 | tf_op jit(solution)/shard_map/all_gather | solution.py:27
  208.9 30.9 %all_gather.90 = bf16[528,1,768]{2,1,0:T(2,128)(2,1)S(1)} all-gather(bf16[132,1,768]{2,1,0:T(2,128)(2,1)S(1)} %copy.220), channel_id=1, replica_groups=mesh['dp'=4,'tensor'=4,'section'=2] {'tensor'}, dimensions={0}, use_global_device_ids=true | all-gather | bytes 1013760 | tf_op jit(solution)/shard_map/all_gather | solution.py:27
  272.5 27.1 %all_gather.91 = bf16[528,1,768]{2,1,0:T(2,128)(2,1)S(1)} all-gather(bf16[132,1,768]{2,1,0:T(2,128)(2,1)S(1)} %copy.222), channel_id=1, replica_groups=mesh['dp'=4,'tensor'=4,'section'=2] {'tensor'}, dimensions={0}, use_global_device_ids=true | all-gather | bytes 1013760 | tf_op jit(solution)/shard_map/all_gather | solution.py:27
  332.7 31.3 %all_gather.92 = bf16[528,1,768]{2,1,0:T(2,128)(2,1)S(1)} all-gather(bf16[132,1,768]{2,1,0:T(2,128)(2,1)S(1)} %copy.223), channel_id=1, replica_groups=mesh['dp'=4,'tensor'=4,'section'=2] {'tensor'}, dimensions={0}, use_global_device_ids=true | all-gather | bytes 1013760 | tf_op jit(solution)/shard_map/all_gather | solution.py:27
  398.7 27.1 %all_gather.93 = bf16[528,1,768]{2,1,0:T(2,128)(2,1)S(1)} all-gather(bf16[132,1,768]{2,1,0:T(2,128)(2,1)S(1)} %copy.225), channel_id=1, replica_groups=mesh['dp'=4,'tensor'=4,'section'=2] {'tensor'}, dimensions={0}, use_global_device_ids=true | all-gather | bytes 1013760 | tf_op jit(solution)/shard_map/all_gather | solution.py:27
  460.8 30.9 %all_gather.94 = bf16[528,1,768]{2,1,0:T(2,128)(2,1)S(1)} all-gather(bf16[132,1,768]{2,1,0:T(2,128)(2,1)S(1)} %copy.226), channel_id=1, replica_groups=mesh['dp'=4,'tensor'=4,'section'=2] {'tensor'}, dimensions={0}, use_global_device_ids=true | all-gather | bytes 1013760 | tf_op jit(solution)/shard_map/all_gather | solution.py:27
  529.1 27.2 %all_gather.95 = bf16[528,1,768]{2,1,0:T(2,128)(2,1)S(1)} all-gather(bf16[132,1,768]{2,1,0:T(2,128)(2,1)S(1)} %copy.228), channel_id=1, replica_groups=mesh['dp'=4,'tensor'=4,'section'=2] {'tensor'}, dimensions={0}, use_global_device_ids=true | all-gather | bytes 1013760 | tf_op jit(solution)/shard_map/all_gather | solution.py:27
  594.3 30.9 %all_gather.96 = bf16[528,1,768]{2,1,0:T(2,128)(2,1)S(1)} all-gather(bf16[132,1,768]{2,1,0:T(2,128)(2,1)S(1)} %copy.229), channel_id=1, replica_groups=mesh['dp'=4,'tensor'=4,'section'=2] {'tensor'}, dimensions={0}, use_global_device_ids=true | all-gather | bytes 1013760 | tf_op jit(solution)/shard_map/all_gather | solution.py:27
  667.6 26.7 %all_gather.97 = bf16[528,1,768]{2,1,0:T(2,128)(2,1)S(1)} all-gather(bf16[132,1,768]{2,1,0:T(2,128)(2,1)S(1)} %copy.231), channel_id=1, replica_groups=mesh['dp'=4,'tensor'=4,'section'=2] {'tensor'}, dimensions={0}, use_global_device_ids=true | all-gather | bytes 1013760 | tf_op jit(solution)/shard_map/all_gather | solution.py:27
  729.5 23.3 %all_gather.98 = bf16[528,1,768]{2,1,0:T(2,128)(2,1)S(1)} all-gather(bf16[132,1,768]{2,1,0:T(2,128)(2,1)S(1)} %copy.232), channel_id=1, replica_groups=mesh['dp'=4,'tensor'=4,'section'=2] {'tensor'}, dimensions={0}, use_global_device_ids=true | all-gather | bytes 1013760 | tf_op jit(solution)/shard_map/all_gather | solution.py:27
  848.8 31.1 %all_gather.100 = bf16[528,1,768]{2,1,0:T(2,128)(2,1)S(1)} all-gather(bf16[132,1,768]{2,1,0:T(2,128)(2,1)S(1)} %copy.237), channel_id=1, replica_groups=mesh['dp'=4,'tensor'=4,'section'=2] {'tensor'}, dimensions={0}, use_global_device_ids=true | all-gather | bytes 1013760 | tf_op jit(solution)/shard_map/all_gather | solution.py:27
  883.8 23.2 %fusion.12 = bf16[136,768]{1,0:T(8,128)(2,1)} fusion(bf16[528,1,768]{2,0,1:T(8,128)(2,1)} %fusion.72), kind=kCustom, calls=%all-reduce-scatter.12 | all-reduce-scatter fusion | flops 417793 | bytes 1020416
  922.9 29.1 %all_gather.101 = bf16[528,1,768]{2,1,0:T(2,128)(2,1)S(1)} all-gather(bf16[132,1,768]{2,1,0:T(2,128)(2,1)S(1)} %copy.238), channel_id=1, replica_groups=mesh['dp'=4,'tensor'=4,'section'=2] {'tensor'}, dimensions={0}, use_global_device_ids=true | all-gather | bytes 1013760 | tf_op jit(solution)/shard_map/all_gather | solution.py:27
  996.0 30.8 %all_gather.102 = bf16[528,1,768]{2,1,0:T(2,128)(2,1)S(1)} all-gather(bf16[132,1,768]{2,1,0:T(2,128)(2,1)S(1)} %copy.242), channel_id=1, replica_groups=mesh['dp'=4,'tensor'=4,'section'=2] {'tensor'}, dimensions={0}, use_global_device_ids=true | all-gather | bytes 1013760 | tf_op jit(solution)/shard_map/all_gather | solution.py:27
  1062.0 26.1 %all_gather.103 = bf16[528,1,768]{2,1,0:T(2,128)(2,1)S(1)} all-gather(bf16[132,1,768]{2,1,0:T(2,128)(2,1)S(1)} %copy.243), channel_id=1, replica_groups=mesh['dp'=4,'tensor'=4,'section'=2] {'tensor'}, dimensions={0}, use_global_device_ids=true | all-gather | bytes 1013760 | tf_op jit(solution)/shard_map/all_gather | solution.py:27
  1128.1 31.1 %all_gather.104 = bf16[528,1,768]{2,1,0:T(2,128)(2,1)S(1)} all-gather(bf16[132,1,768]{2,1,0:T(2,128)(2,1)S(1)} %copy.247), channel_id=1, replica_groups=mesh['dp'=4,'tensor'=4,'section'=2] {'tensor'}, dimensions={0}, use_global_device_ids=true | all-gather | bytes 1013760 | tf_op jit(solution)/shard_map/all_gather | solution.py:27
  1191.4 26.4 %all_gather.105 = bf16[528,1,768]{2,1,0:T(2,128)(2,1)S(1)} all-gather(bf16[132,1,768]{2,1,0:T(2,128)(2,1)S(1)} %copy.248), channel_id=1, replica_groups=mesh['dp'=4,'tensor'=4,'section'=2] {'tensor'}, dimensions={0}, use_global_device_ids=true | all-gather | bytes 1013760 | tf_op jit(solution)/shard_map/all_gather | solution.py:27
  1255.7 31.5 %all_gather.106 = bf16[528,1,768]{2,1,0:T(2,128)(2,1)S(1)} all-gather(bf16[132,1,768]{2,1,0:T(2,128)(2,1)S(1)} %copy.252), channel_id=1, replica_groups=mesh['dp'=4,'tensor'=4,'section'=2] {'tensor'}, dimensions={0}, use_global_device_ids=true | all-gather | bytes 1013760 | tf_op jit(solution)/shard_map/all_gather | solution.py:27
  1291.1 23.1 %fusion.18 = bf16[136,768]{1,0:T(8,128)(2,1)} fusion(bf16[528,1,768]{2,0,1:T(8,128)(2,1)} %fusion.75), kind=kCustom, calls=%all-reduce-scatter.18 | all-reduce-scatter fusion | flops 417793 | bytes 1020416
  1321.7 29.0 %all_gather.107 = bf16[528,1,768]{2,1,0:T(2,128)(2,1)S(1)} all-gather(bf16[132,1,768]{2,1,0:T(2,128)(2,1)S(1)} %copy.253), channel_id=1, replica_groups=mesh['dp'=4,'tensor'=4,'section'=2] {'tensor'}, dimensions={0}, use_global_device_ids=true | all-gather | bytes 1013760 | tf_op jit(solution)/shard_map/all_gather | solution.py:27
  1461.7 26.2 %reduce-scatter.86.cloned.1.call-done = bf16[192,192]{1,0:T(8,128)(2,1)} async-done(((bf16[768,192]{1,0:T(8,128)(2,1)}), bf16[192,192]{1,0:T(8,128)(2,1)}) %reduce-scatter.86.cloned.1.call-update) | async-done | bytes 73744
  1489.8 28.5 %reduce-scatter.84.cloned.1.call-done = bf16[192,576]{1,0:T(8,128)(2,1)} async-done(((bf16[768,576]{1,0:T(8,128)(2,1)}), bf16[192,576]{1,0:T(8,128)(2,1)}) %reduce-scatter.84.cloned.1.call-update) | async-done | bytes 221200
  1520.6 29.1 %reduce-scatter.88.cloned.1.call-done = bf16[192,768]{1,0:T(8,128)(2,1)} async-done(((bf16[768,768]{1,0:T(8,128)(2,1)}), bf16[192,768]{1,0:T(8,128)(2,1)}) %reduce-scatter.88.cloned.1.call-update) | async-done | bytes 294928
  1552.5 28.7 %reduce-scatter.80.cloned.1.call-done = bf16[1,192,768]{2,1,0:T(8,128)(2,1)} async-done(((bf16[1,768,768]{2,1,0:T(8,128)(2,1)}), bf16[1,192,768]{2,1,0:T(8,128)(2,1)}) %reduce-scatter.80.cloned.1.call-update) | async-done | bytes 294928 | tf_op jit(solution)/shard_map/reduce_scatter | solution.py:329
  (989 shorter events, 889.7 us)
Async XLA Ops:
  7.2 170.6 %all-gather.4.cloned.1.call-start = ((), (), s32[]{:S(2)}) async-start(), calls=%async_computation.7 | async-start | bytes 1474560 | tf_op jit(solution)/shard_map/all_gather | solution.py:228
  9.1 172.5 %all-gather.6.cloned.1.call-start = ((), (), s32[]{:S(2)}) async-start(), calls=%async_computation.8 | async-start | bytes 1474560 | tf_op jit(solution)/shard_map/all_gather | solution.py:229
  121.2 35.7 %collective-permute-start.13 = (bf16[12,768]{1,0:T(8,128)(2,1)S(1)}, bf16[12,768]{1,0:T(8,128)(2,1)S(1)}, u32[]{:S(2)}, u32[]{:S(2)}) collective-permute-start(bf16[12,768]{1,0:T(8,128)(2,1)S(1)} %slice.299), channel_id=1, source_target_pairs={{0,2},{2,4},{4,6},{1,3},{3,5},{5,7},{8,10},{10,12},{12,14},{9,11},... | collective-permute-start | bytes 55304
  123.3 1318.9 %reduce-scatter.92.cloned.1.call-start = ((), (), s32[]{:S(2)}) async-start(), calls=%async_computation.15 | async-start | bytes 245760
  325.5 5.7 collective-permute-start.1
  328.1 4.1 collective-permute-start.2
  453.1 6.2 collective-permute-start.3
  521.6 4.8 collective-permute-start.19
  586.8 5.1 collective-permute-start.5
  776.6 5.1 collective-permute-start.23
  841.6 5.5 collective-permute-start.7
  907.8 7.5 collective-permute-start.25
  986.5 6.6 collective-permute-start.9
  1053.2 6.5 collective-permute-start.27
  1118.5 6.4 collective-permute-start.11
  1185.6 4.2 collective-permute-start.29
  1249.6 5.1 collective-permute-start.12
  1315.0 4.1 collective-permute-start.31
  1374.3 69.4 %reduce-scatter.90.cloned.1.call-start = ((), (), s32[]{:S(2)}) async-start(), calls=%async_computation.14 | async-start | bytes 245760
  1398.4 61.8 %reduce-scatter.82.cloned.1.call-start = ((), (), s32[]{:S(2)}) async-start(), calls=%async_computation.10 | async-start | bytes 442368
  1401.5 86.4 %reduce-scatter.86.cloned.1.call-start = ((), (), s32[]{:S(2)}) async-start(), calls=%async_computation.12 | async-start | bytes 491520
  1404.0 114.2 %reduce-scatter.84.cloned.1.call-start = ((), (), s32[]{:S(2)}) async-start(), calls=%async_computation.11 | async-start | bytes 1228800
  1413.0 136.7 %reduce-scatter.88.cloned.1.call-start = ((), (), s32[]{:S(2)}) async-start(), calls=%async_computation.13 | async-start | bytes 1474560
  1430.3 150.9 %reduce-scatter.80.cloned.1.call-start = ((), (), s32[]{:S(2)}) async-start(), calls=%async_computation.9 | async-start | bytes 1474560 | tf_op jit(solution)/shard_map/reduce_scatter | solution.py:329
  (263 other events, 3576.2 us)
Sparse Core Ops, SparseCore 0:
  9.8 34.6 all-gather.3
  123.5 26.8 all-gather.5
  1374.5 21.1 reduce-scatter.91
  1398.9 23.9 reduce-scatter.89
  1426.4 33.8 reduce-scatter.81
  1463.5 24.4 reduce-scatter.85
  1490.9 27.2 reduce-scatter.83
  1521.1 28.5 reduce-scatter.87
  1552.6 28.5 reduce-scatter.79
where the time goes:
time: 1600 us; the launch traced here: 1590 us
  blocking collectives  1040 us (65%)
  waiting for transfers between devices  142 us (9%)
  matrix products  127 us (8%)
  local copies, waits for them, and re-layouts  124 us (8%)
  other arithmetic  73.7 us (5%)
  starting transfers between devices  57.8 us (4%)
  between operations  21.4 us (1%)
    all_gather x20, blocking collectives, gather_rows(): return lax.all_gather(values, 'tensor', axis=0, tiled=True)  558 us
    unnamed x20, blocking collectives  404 us
    unnamed x35, waiting for transfers between devices  106 us
    unnamed x558, local copies, waits for them, and re-layouts  93.4 us
    unnamed x26, starting transfers between devices  34.7 us
  transfers between devices with their start and end apart: 42, of which 20 were waited for; matrix products, arithmetic and copies ran while one was open for 11% of the time, Pallas kernels for 0%

commit v1 on v0

v1 whole, which is shorter than its diff:
```python
import functools

import jax
import jax.numpy as jnp
from jax import lax
from jax.experimental import pallas as pl
from jax.experimental.pallas import tpu as pltpu
from jax.sharding import PartitionSpec as P

HEAD = 64
LOW = jnp.bfloat16
WIDE = jnp.float32
PAIR = 2 * HEAD


def swap(block, axis, mask):
    return lax.ppermute(block, axis, [(i, i ^ mask) for i in range(lax.axis_size(axis))])


def route(block, pairs_of):
    tensor_count, section_count = (lax.axis_size("tensor"), lax.axis_size("section"))
    pairs = []
    for t in range(tensor_count):
        for s in range(section_count):
            to = pairs_of(t, s)
            if to is not None:
                pairs.append((t * section_count + s, to[0] * section_count + to[1]))
    return lax.ppermute(block, ("tensor", "section"), pairs)


def dot(left, right, contract):
    return lax.dot_general(left, right, (contract, ((), ())), preferred_element_type=WIDE)


def nn(left, right):
    return dot(left, right, ((1,), (0,)))


def nt(left, right):
    return dot(left, right, ((1,), (1,)))


def tn(left, right):
    return dot(left, right, ((0,), (0,)))


def bits_of(count):
    return count.bit_length() - 1


def own_order(values):
    count = lax.axis_size("dp")
    place = lax.axis_index("dp")
    width = values.shape[-1]
    lead = values.shape[:-1]
    for bit in range(bits_of(count)):
        step = 1 << bit
        cut = values.reshape(lead + (count // (2 * step), 2, width * step // count))
        turned = jnp.concatenate([cut[..., 1:2, :], cut[..., 0:1, :]], -2).reshape(values.shape)
        values = jnp.where((place >> bit) & 1 == 1, turned, values)
    return values


def gather_pair(first, second):
    for mask in (2, 1):
        width = first.shape[1]
        came = swap(jnp.concatenate([first, second], 1), "tensor", mask)
        first = jnp.concatenate([first, came[:, :width]], 1)
        second = jnp.concatenate([second, came[:, width:]], 1)
    count = bits_of(lax.axis_size("dp"))
    rows, width = first.shape
    first = first.reshape((1,) * count + first.shape)
    second = second.reshape((1,) * count + second.shape)
    for step in range(count):
        low, high = (step, count - 1 - step)
        came_first = swap(first, "dp", 1 << low)
        came_second = swap(second, "dp", 1 << high)
        first = jnp.concatenate([first, came_first], count - 1 - low)
        second = jnp.concatenate([second, came_second], count - 1 - high)
    full = (rows << count, width)
    return (first.reshape(full), second.reshape(full))


def scatter_pair(first, second):
    count = bits_of(lax.axis_size("dp"))
    rows, width = first.shape
    cut = (2,) * count + (rows >> count, width)
    first = first.reshape(cut)
    second = second.reshape(cut)

    def halves(block, axis):
        return (lax.slice_in_dim(block, 0, 1, axis=axis), lax.slice_in_dim(block, 1, 2, axis=axis))

    for step in range(count):
        high, low = (count - 1 - step, step)
        keep_first, send_first = halves(first, count - 1 - high)
        keep_second, send_second = halves(second, count - 1 - low)
        came_first = swap(send_first, "dp", 1 << high)
        came_second = swap(send_second, "dp", 1 << low)
        first = add_low(keep_first, came_first)
        second = add_low(keep_second, came_second)
    first = first.reshape(rows >> count, width)
    second = second.reshape(rows >> count, width)
    for mask in (1, 2):
        half = first.shape[1] // 2
        came = swap(jnp.concatenate([first[:, half:], second[:, half:]], 1), "tensor", mask)
        first = add_low(first[:, :half], came[:, :half])
        second = add_low(second[:, :half], came[:, half:])
    return (first, second)


def add_low(left, right):
    return (left.astype(WIDE) + right.astype(WIDE)).astype(LOW)


def norm_forward(values, gain, shift):
    centred = values - jnp.mean(values, -1, keepdims=True)
    scale = lax.rsqrt(jnp.mean(centred * centred, -1, keepdims=True) + 1e-05)
    plain = centred * scale
    return (plain * gain + shift, plain, scale)


def norm_backward(grad, plain, scale, gain):
    inner = grad * gain
    mean_inner = jnp.mean(inner, -1, keepdims=True)
    mean_along = jnp.mean(inner * plain, -1, keepdims=True)
    return (
        scale * (inner - mean_inner - plain * mean_along),
        jnp.sum(grad * plain, 0),
        jnp.sum(grad, 0),
    )


def attention_kernel(q_ref, k_ref, v_ref, allowed_ref, mixed_ref, mass_ref):
    queries, keys, values = (q_ref[...], k_ref[...], v_ref[...])
    allowed = allowed_ref[...] > 0
    lower = lax.broadcasted_iota(jnp.int32, queries.shape, 1) < HEAD
    mixed, mass = ([], [])
    for side in (lower, ~lower):
        scores = nt(jnp.where(side, queries, jnp.zeros_like(queries)), keys) * HEAD ** (-0.5)
        scores = jnp.where(allowed, scores, -1e9)
        top = jnp.max(scores, -1, keepdims=True)
        raised = jnp.exp(scores - top)
        total = jnp.sum(raised, -1, keepdims=True)
        mixed.append(nn((raised / total).astype(LOW), values))
        mass.append(top + jnp.log(total))
    mixed_ref[...] = jnp.where(lower, mixed[0], mixed[1]).astype(LOW)
    mass_ref[...] = jnp.where(lower, mass[0], mass[1])


def attention_back_kernel(
    q_ref, k_ref, v_ref, allowed_ref, grad_ref, mass_ref, gq_ref, gk_ref, gv_ref
):
    queries, keys, values, grad = (q_ref[...], k_ref[...], v_ref[...], grad_ref[...])
    allowed = allowed_ref[...] > 0
    mass = mass_ref[...]
    lower = lax.broadcasted_iota(jnp.int32, queries.shape, 1) < HEAD
    lower_keys = lax.broadcasted_iota(jnp.int32, keys.shape, 1) < HEAD
    scale = HEAD ** (-0.5)
    none = jnp.zeros_like(queries)
    grad_q, grad_k, grad_v = ([], [], [])
    for side, column in ((lower, 0), (~lower, HEAD)):
        scores = nt(jnp.where(side, queries, none), keys) * scale
        probs = jnp.where(allowed, jnp.exp(scores - mass[:, column : column + 1]), 0.0)
        grad_probs = nt(jnp.where(side, grad, none), values)
        inner = jnp.sum(probs * grad_probs, -1, keepdims=True)
        grad_scores = (probs * (grad_probs - inner)).astype(LOW)
        grad_q.append(nn(grad_scores, keys) * scale)
        grad_k.append(tn(grad_scores, queries) * scale)
        grad_v.append(tn(probs.astype(LOW), grad))
    gq_ref[...] = jnp.where(lower, grad_q[0], grad_q[1]).astype(LOW)
    gk_ref[...] = jnp.where(lower_keys, grad_k[0], grad_k[1]).astype(LOW)
    gv_ref[...] = jnp.where(lower_keys, grad_v[0], grad_v[1]).astype(LOW)


def attention_specs(rows, keys):
    row_spec = pl.BlockSpec((rows, PAIR), lambda i: (0, i))
    key_spec = pl.BlockSpec((keys, PAIR), lambda i: (0, i))
    allowed_spec = pl.BlockSpec((rows, keys), lambda i: (0, 0))
    return (row_spec, key_spec, allowed_spec)


def attention(queries, keys, values, allowed):
    rows, width = queries.shape
    row_spec, key_spec, allowed_spec = attention_specs(rows, keys.shape[0])
    work = 4 * rows * keys.shape[0] * width
    return pl.pallas_call(
        attention_kernel,
        grid=(width // PAIR,),
        in_specs=[row_spec, key_spec, key_spec, allowed_spec],
        out_specs=[row_spec, row_spec],
        out_shape=[
            jax.ShapeDtypeStruct((rows, width), LOW),
            jax.ShapeDtypeStruct((rows, width), WIDE),
        ],
        cost_estimate=pl.CostEstimate(flops=2 * work, bytes_accessed=4000000, transcendentals=0),
    )(queries, keys, values, allowed)


def attention_back(queries, keys, values, allowed, grad, mass):
    rows, width = queries.shape
    row_spec, key_spec, allowed_spec = attention_specs(rows, keys.shape[0])
    work = 10 * rows * keys.shape[0] * width
    return pl.pallas_call(
        attention_back_kernel,
        grid=(width // PAIR,),
        in_specs=[row_spec, key_spec, key_spec, allowed_spec, row_spec, row_spec],
        out_specs=[row_spec, key_spec, key_spec],
        out_shape=[
            jax.ShapeDtypeStruct((rows, width), LOW),
            jax.ShapeDtypeStruct(keys.shape, LOW),
            jax.ShapeDtypeStruct(keys.shape, LOW),
        ],
        cost_estimate=pl.CostEstimate(flops=2 * work, bytes_accessed=6000000, transcendentals=0),
    )(queries, keys, values, allowed, grad, mass)


def layer_forward(rows, key_rows, allowed, weights, gains, shifts):
    (w_q, w_k, w_v, w_out), expand, reduce = weights
    queries = nn(rows, w_q).astype(LOW)
    keys = nn(key_rows, w_k).astype(LOW)
    values = nn(key_rows, w_v).astype(LOW)
    mixed, mass = attention(queries, keys, values, allowed)
    first_sum = rows.astype(WIDE) + nt(mixed, w_out)
    normed, plain_one, scale_one = norm_forward(first_sum, gains[0], shifts[0])
    normed_low = normed.astype(LOW)
    hidden = [nn(normed_low, part) for part in expand]
    active = [
        (0.5 * part * (1.0 + lax.erf(part * 0.7071067811865476))).astype(LOW) for part in hidden
    ]
    second_sum = normed + sum(nt(act, part) for act, part in zip(active, reduce))
    result, plain_two, scale_two = norm_forward(second_sum, gains[1], shifts[1])
    kept = (
        (rows, key_rows, queries, keys, values, mixed, mass, allowed),
        (plain_one, scale_one, normed_low, hidden, active, plain_two, scale_two),
    )
    return (result.astype(LOW), kept)


def layer_backward(grad_out, kept, weights, gains):
    (w_q, w_k, w_v, w_out), expand, reduce = weights
    (rows, key_rows, queries, keys, values, mixed, mass, allowed) = kept[0]
    (plain_one, scale_one, normed_low, hidden, active, plain_two, scale_two) = kept[1]
    grad_second, gain_two, shift_two = norm_backward(
        grad_out.astype(WIDE), plain_two, scale_two, gains[1]
    )
    grad_ffn = grad_second.astype(LOW)
    grad_hidden = []
    for part, hid in zip(reduce, hidden):
        slope = 0.5 * (1.0 + lax.erf(hid * 0.7071067811865476)) + hid * (
            0.3989422804014327 * jnp.exp(-0.5 * hid * hid)
        )
        grad_hidden.append((nn(grad_ffn, part) * slope).astype(LOW))
    grad_normed = grad_second + sum(nt(grad, part) for grad, part in zip(grad_hidden, expand))
    grad_first, gain_one, shift_one = norm_backward(grad_normed, plain_one, scale_one, gains[0])
    grad_attn = grad_first.astype(LOW)
    grad_mixed = nn(grad_attn, w_out).astype(LOW)
    grad_q, grad_k, grad_v = attention_back(queries, keys, values, allowed, grad_mixed, mass)
    key_part = nt(grad_k, w_k) + nt(grad_v, w_v)
    own_part = grad_first + nt(grad_q, w_q)
    terms = (
        (rows, key_rows, grad_q, grad_k, grad_v, mixed, grad_attn),
        (normed_low, grad_hidden, active, grad_ffn),
    )
    norm_terms = jnp.stack([gain_one, gain_two, shift_one, shift_two], 0)
    return (own_part, key_part, terms, norm_terms)


def gather_keys(tokens):
    across = swap(tokens, "tensor", 1)
    return [tokens, swap(tokens, "section", 1), across, swap(across, "section", 1)]


def collect_rows(own_part, key_part, quarter):
    mine = own_part[:quarter] + key_part[:quarter]
    beside = key_part[quarter : 2 * quarter]
    across = key_part[2 * quarter : 3 * quarter]
    far = key_part[3 * quarter : 4 * quarter]
    memory = own_part[quarter:] + key_part[4 * quarter :]
    came = swap(jnp.concatenate([beside, far, memory], 0).astype(LOW), "section", 1).astype(WIDE)
    mine = mine + came[:quarter]
    across = across + came[quarter : 2 * quarter]
    memory = memory + came[2 * quarter :]
    came = swap(jnp.concatenate([across, memory], 0).astype(LOW), "tensor", 1).astype(WIDE)
    return ((mine + came[:quarter]).astype(LOW), (memory + came[quarter:]).astype(LOW))


def shards(
    tokens,
    cotangent,
    document_starts,
    valid_count,
    reset_flags,
    memory_init,
    attention_in,
    attention_out,
    feed_expand,
    feed_reduce,
    norm_gains,
    norm_shifts,
):
    dp_count, tensor_count, section_count = (lax.axis_size(a) for a in ("dp", "tensor", "section"))
    dp_place, tensor_place = (lax.axis_index("dp"), lax.axis_index("tensor"))
    first_section = lax.axis_index("section") == 0
    first_group = tensor_place // 2 == 0
    counts_memory = first_section & (tensor_place % 2 == 0)
    segments, quarter, width = tokens.shape[1:]
    memory_count = memory_init.shape[0] * tensor_count
    block = attention_in.shape[1]
    unit_half = feed_expand.shape[2] // 2

    def by_section(at_first, at_second):
        return jnp.where(first_section, at_first, at_second)

    def of_group(array):
        return jnp.where(first_group, array[0], array[1])

    def of_other(array):
        return jnp.where(first_group, array[1], array[0])

    def quarter_rows(array):
        came = route(of_other(array), lambda t, s: (t ^ 2, 1) if s == 1 else None)
        return own_order(by_section(of_group(array), came))

    token_parts = [gather_keys(quarter_rows(tokens[:, 0]))]

    small = jnp.concatenate(
        [memory_init.reshape(-1), norm_gains.reshape(-1), norm_shifts.reshape(-1)]
    ).astype(LOW)
    small = lax.all_gather(small, ("dp", "tensor", "section"), axis=0, tiled=False)
    small = small.reshape(dp_count, tensor_count, section_count, -1)
    memory_size = memory_init.size
    init_rows = small[..., :memory_size].reshape(
        dp_count, tensor_count, section_count, memory_init.shape[0], memory_init.shape[1]
    )
    init_rows = own_order(init_rows.transpose(1, 3, 0, 2, 4).reshape(memory_count, width))
    norm_rows = small[:, 0, :, memory_size:].reshape(dp_count, section_count, 4, block)
    norm_rows = norm_rows.transpose(1, 2, 0, 3).reshape(section_count, 4, width)
    norm_rows = own_order(norm_rows).astype(WIDE)
    gains = norm_rows[:, 0:2]
    shifts = norm_rows[:, 2:4]

    low_in = attention_in[0].astype(LOW)
    low_out = attention_out[0].astype(LOW).T
    low_expand = feed_expand[0].astype(LOW)
    low_reduce = feed_reduce[0].astype(LOW).T
    halves = (
        jnp.concatenate(
            [low_in[:, 0], low_in[:, 1], low_expand[:, :unit_half], low_reduce[:, :unit_half]], 1
        ),
        jnp.concatenate(
            [low_in[:, 2], low_out, low_expand[:, unit_half:], low_reduce[:, unit_half:]], 1
        ),
    )
    mine = by_section(halves[0], halves[1])
    came = swap(by_section(halves[1], halves[0]), "section", 1)
    layer_shards = (by_section(mine, came), by_section(came, mine))
    cols = low_out.shape[1]
    weights = []
    for shard in layer_shards:
        one, two = gather_pair(shard[:, :cols], shard[:, cols : 2 * cols])
        came_one, came_two = (swap(one, "section", 1), swap(two, "section", 1))
        attention_weights = (
            by_section(one, came_one),
            by_section(two, came_two),
            by_section(came_one, one),
            by_section(came_two, two),
        )
        expand, reduce = gather_pair(
            shard[:, 2 * cols : 2 * cols + unit_half], shard[:, 2 * cols + unit_half :]
        )
        weights.append(
            (
                attention_weights,
                (expand, swap(expand, "section", 1)),
                (reduce, swap(reduce, "section", 1)),
            )
        )

    starts, valid, resets = (of_group(document_starts), of_group(valid_count), of_group(reset_flags))
    for segment in range(1, segments):
        token_parts.append(gather_keys(quarter_rows(tokens[:, segment])))
    grad_ends = [quarter_rows(cotangent[:, segment]) for segment in range(segments)]

    def places(across, beside):
        at = tensor_place ^ across
        at = by_section(at ^ (2 * beside), at ^ (2 * (1 - beside)))
        return at * quarter + jnp.arange(quarter)

    memory_places = jnp.full((memory_count,), -1)
    row_places = jnp.concatenate([places(0, 0), memory_places])
    key_places = jnp.concatenate(
        [places(0, 0), places(0, 1), places(1, 0), places(1, 1), memory_places]
    )

    def allowed_of(segment):
        row_doc = jnp.sum(starts[segment][None, :] <= row_places[:, None], -1)
        key_doc = jnp.sum(starts[segment][None, :] <= key_places[:, None], -1)
        live = key_places < valid[segment]
        either = (row_places < 0)[:, None] | (key_places < 0)[None, :]
        return (live[None, :] & (either | (row_doc[:, None] == key_doc[None, :]))).astype(WIDE)

    kept = []
    ends = []
    memory_rows = init_rows
    for segment in range(segments):
        if segment > 0:
            memory_rows = jnp.where(resets[segment - 1] > 0, init_rows, memory_rows)
        allowed = allowed_of(segment)
        parts = token_parts[segment]
        kept.append([])
        for layer in range(2):
            rows = jnp.concatenate([parts[0], memory_rows], 0)
            key_rows = jnp.concatenate(parts + [memory_rows], 0)
            result, state = layer_forward(
                rows, key_rows, allowed, weights[layer], gains[layer], shifts[layer]
            )
            kept[segment].append(state)
            memory_rows = result[quarter:]
            if layer == 0:
                parts = gather_keys(result[:quarter])
        ends.append(result[:quarter])

    token_grads = [None] * segments
    terms = [[None] * segments for _ in range(2)]
    norm_sums = [0.0, 0.0]
    memory_sum = jnp.zeros((memory_count, width), WIDE)
    memory_grad = jnp.zeros((memory_count, width), LOW)
    for segment in reversed(range(segments)):
        live = places(0, 0) < valid[segment]
        token_grad = jnp.where(live[:, None], grad_ends[segment], jnp.zeros_like(grad_ends[segment]))
        for layer in (1, 0):
            grad_out = jnp.concatenate([token_grad, memory_grad], 0)
            own_part, key_part, terms[layer][segment], norm_terms = layer_backward(
                grad_out, kept[segment][layer], weights[layer], gains[layer]
            )
            norm_sums[layer] = norm_sums[layer] + norm_terms
            token_grad, memory_grad = collect_rows(own_part, key_part, quarter)
            memory_grad = jnp.where(counts_memory, memory_grad, jnp.zeros_like(memory_grad))
        token_grads[segment] = token_grad
        wide_grad = memory_grad.astype(WIDE)
        if segment > 0:
            reset = resets[segment - 1] > 0
            memory_sum = memory_sum + jnp.where(reset, wide_grad, 0.0)
            memory_grad = jnp.where(reset, jnp.zeros_like(memory_grad), memory_grad)
        else:
            memory_sum = memory_sum + wide_grad

    def stacked(layer, which, index):
        return jnp.concatenate([term[which][index] for term in terms[layer]], 0)

    owned = [None, None]
    for layer in (1, 0):
        normed_low = stacked(layer, 1, 0)
        grad_ffn = stacked(layer, 1, 3)
        grad_hidden, active = (
            [jnp.concatenate([term[1][which][half] for term in terms[layer]], 0) for half in (0, 1)]
            for which in (1, 2)
        )
        expand_own, expand_send = (tn(normed_low, part).astype(LOW) for part in grad_hidden)
        reduce_own, reduce_send = (tn(grad_ffn, part).astype(LOW) for part in active)
        expand, reduce = scatter_pair(
            add_low(expand_own, swap(expand_send, "section", 1)),
            add_low(reduce_own, swap(reduce_send, "section", 1)),
        )
        rows, key_rows, grad_q, grad_k, grad_v, mixed, grad_attn = (
            stacked(layer, 0, index) for index in range(7)
        )
        grads = [
            tn(rows, grad_q).astype(LOW),
            tn(key_rows, grad_k).astype(LOW),
            tn(key_rows, grad_v).astype(LOW),
            tn(grad_attn, mixed).astype(LOW),
        ]
        one, two = scatter_pair(
            *(
                add_low(
                    by_section(grads[place], grads[place + 2]),
                    swap(by_section(grads[place + 2], grads[place]), "section", 1),
                )
                for place in (0, 1)
            )
        )
        owned[layer] = jnp.concatenate([one, two, expand, reduce], 1)
    came = swap(by_section(owned[1], owned[0]), "section", 1)
    first_half = by_section(owned[0], came).astype(WIDE)
    second_half = by_section(came, owned[1]).astype(WIDE)

    def cut(array, place):
        if place < 2:
            return array[:, place * cols : (place + 1) * cols]
        start = 2 * cols + (place - 2) * unit_half
        return array[:, start : start + unit_half]

    in_grad = jnp.stack([cut(first_half, 0), cut(first_half, 1), cut(second_half, 0)], 1)[None]
    out_grad = cut(second_half, 1).T[None]
    expand_grad = jnp.concatenate([cut(first_half, 2), cut(second_half, 2)], 1)[None]
    reduce_grad = jnp.concatenate([cut(first_half, 3), cut(second_half, 3)], 1).T[None]

    sums = own_order(jnp.concatenate([memory_sum, norm_sums[0], norm_sums[1]], 0))
    sums = lax.psum(sums, ("dp", "tensor", "section"))
    memory_cols = memory_init.shape[1]
    memory_grad = lax.dynamic_slice(
        sums,
        (
            tensor_place * memory_init.shape[0],
            (dp_place * section_count + lax.axis_index("section")) * memory_cols,
        ),
        memory_init.shape,
    )
    norm_grads = lax.dynamic_slice(
        by_section(sums[memory_count : memory_count + 4], sums[memory_count + 4 :]),
        (0, dp_place * block),
        (4, block),
    )

    outs = jnp.stack(ends, 0)
    grads = jnp.stack(token_grads, 0)
    out_near = route(outs, lambda t, s: (t, 1) if s == 0 else None)
    out_far = route(outs, lambda t, s: (t ^ 2, 1) if s == 1 else None)
    grad_far = route(grads, lambda t, s: (t ^ 2, 0) if s == 1 else None)
    near = by_section(grads, out_near)
    far = by_section(grad_far, out_far)
    layer_ends = own_order(
        jnp.stack([jnp.where(first_group, near, far), jnp.where(first_group, far, near)], 0)
    )[None]
    return (
        layer_ends,
        memory_grad,
        in_grad,
        out_grad,
        expand_grad,
        reduce_grad,
        norm_grads[None, 0:2],
        norm_grads[None, 2:4],
    )


def solution(mesh):
    in_specs = (
        P("dp", None, "tensor", None),
        P("dp", None, "tensor", None),
        P("dp", None, None),
        P("dp", None),
        P("dp", None),
        P("tensor", ("dp", "section")),
        P("section", "dp", None, "tensor"),
        P("section", "tensor", "dp"),
        P("section", "dp", "tensor"),
        P("section", "tensor", "dp"),
        P("section", None, "dp"),
        P("section", None, "dp"),
    )
    out_specs = (
        P("section", "dp", None, "tensor", None),
        P("tensor", ("dp", "section")),
        P("section", "dp", None, "tensor"),
        P("section", "tensor", "dp"),
        P("section", "dp", "tensor"),
        P("section", "tensor", "dp"),
        P("section", None, "dp"),
        P("section", None, "dp"),
    )
    return jax.shard_map(shards, mesh=mesh, in_specs=in_specs, out_specs=out_specs, check_vma=False)
```

time: 1600 us -> 953 us (0.60)
  blocking collectives: 1040 us -> 47.9 us
  waiting for transfers between devices: 142 us -> 404 us
  Pallas kernels: 0 us -> 72 us
  local copies, waits for them, and re-layouts: 124 us -> 87.2 us
  other arithmetic: 73.7 us -> 96.9 us
  matrix products: 127 us -> 144 us
    all_gather x25 -> x1, blocking collectives: 623 us -> 47.9 us  [shards(): lax.all_gather(small, ('dp', 'tensor', 'section'), axis=0, tiled=False)]
    unnamed x20 -> x0, blocking collectives: 404 us -> none
    ppermute x13 -> x93, waiting for transfers between devices: 7.77 us -> 286 us  [the longest x86 286 us: swap(): lax.ppermute(block, axis, [(i, i ^ mask) for i in range(lax.axis_size(axi...]
    psum x0 -> x1, waiting for transfers between devices: none -> 118 us  [shards(): sums = lax.psum(sums, ('dp', 'tensor', 'section'))]
    unnamed x35 -> x1, waiting for transfers between devices: 106 us -> 0.02 us
    pallas_call x0 -> x8, Pallas kernels: none -> 72 us  [the longest x4 39.8 us: attention_back(): pl.pallas_call(attention_back_kernel, grid=(width // PAIR,), in_specs=[ro...]
    unnamed x558 -> x596, local copies, waits for them, and re-layouts: 93.4 us -> 31.8 us
    ppermute x13 -> x93, starting transfers between devices: 22.8 us -> 67.4 us  [the longest x86 58.6 us: swap(): lax.ppermute(block, axis, [(i, i ^ mask) for i in range(lax.axis_size(axi...]
  transfers between devices with their start and end apart: 42 -> 94, of which waited for: 20 -> 42; matrix products, arithmetic and copies ran while one was open for 11% -> 23% of each run, Pallas kernels for 0% -> 4%
where the time goes in v1:
time: 953 us; the launch traced here: 940 us
  waiting for transfers between devices  404 us (42%)
  matrix products  144 us (15%)
  other arithmetic  96.9 us (10%)
  local copies, waits for them, and re-layouts  87.2 us (9%)
  Pallas kernels  72 us (8%)
  starting transfers between devices  67.5 us (7%)
  blocking collectives  47.9 us (5%)
  between operations  20.7 us (2%)
    ppermute x86, waiting for transfers between devices, swap(): lax.ppermute(block, axis, [(i, i ^ mask) for i in range(lax.axis_size(axi...  286 us
    dot_general x80, matrix products, dot(): lax.dot_general(left, right, (contract, ((), ())), preferred_element_type...  144 us
    psum x1, waiting for transfers between devices, shards(): sums = lax.psum(sums, ('dp', 'tensor', 'section'))  118 us
    ppermute x86, starting transfers between devices, swap(): lax.ppermute(block, axis, [(i, i ^ mask) for i in range(lax.axis_size(axi...  58.6 us
    all_gather x1, blocking collectives, shards(): lax.all_gather(small, ('dp', 'tensor', 'section'), axis=0, tiled=False)  47.9 us
    pallas_call x4, Pallas kernels, attention_back(): pl.pallas_call(attention_back_kernel, grid=(width // PAIR,), in_specs=[ro...  39.8 us
    pallas_call x4, Pallas kernels, attention(): pl.pallas_call(attention_kernel, grid=(width // PAIR,), in_specs=[row_spe...  32.3 us
    unnamed x596, local copies, waits for them, and re-layouts  31.8 us
  transfers between devices with their start and end apart: 94, of which 42 were waited for; matrix products, arithmetic and copies ran while one was open for 23% of the time, Pallas kernels for 4%

profile of v1, /device:TPU:0, one launch (start us, length us, event | category | flops | bytes accessed | tf_op | source)
XLA Modules:
  0.0 939.7 jit_solution(1936655583872180456)
XLA Ops:
  16.5 47.9 %all-gather = bf16[32,1,1152]{2,1,0:T(2,128)(2,1)S(1)} all-gather(bf16[1,1,1152]{2,1,0:T(2,128)(2,1)S(1)} %maximum_bitcast_fusion.11), channel_id=1, replica_groups=mesh['dp'=4,'tensor'=4,'section'=2] {'dp','tensor','section'}, dimensions={0}, use_global_device_ids=true | all-gather | bytes 76032 | tf_op jit(solution)/shard_map/all_gather | solution.py:330
  98.3 31.1 %collective-permute-done.2 = bf16[192,384]{1,0:T(8,128)(2,1)S(1)} collective-permute-done((bf16[192,384]{1,0:T(8,128)(2,1)S(1)}, bf16[192,384]{1,0:T(8,128)(2,1)S(1)}, u32[]{:S(2)}, u32[]{:S(2)}) %collective-permute-start.2) | collective-permute-done | bytes 147488 | tf_op jit(solution)/shard_map/ppermute | solution.py:17
  179.9 11.5 %collective-permute-done.24 = bf16[1,2,192,768]{3,2,1,0:T(8,128)(2,1)S(1)} collective-permute-done((bf16[1,2,192,768]{3,2,1,0:T(8,128)(2,1)S(1)}, bf16[1,2,192,768]{3,2,1,0:T(8,128)(2,1)S(1)}, u32[]{:S(2)}, u32[]{:S(2)}) %collective-permute-start.24) | collective-permute-done | bytes 589856 | tf_op jit(solution)/shard_map/ppermute | solution.py:17
  194.8 7.4 collective-permute-done.34
  223.5 8.0 shard_map.179
  233.1 7.2 collective-permute-done.16
  251.8 15.6 %collective-permute-done.37 = bf16[2,1,192,1536]{3,2,1,0:T(8,128)(2,1)} collective-permute-done((bf16[2,1,192,1536]{3,2,1,0:T(8,128)(2,1)}, bf16[2,1,192,1536]{3,2,1,0:T(8,128)(2,1)}, u32[]{:S(2)}, u32[]{:S(2)}) %collective-permute-start.37) | collective-permute-done | bytes 1179680 | tf_op jit(solution)/shard_map/ppermute | solution.py:17
  296.0 8.0 shard_map.180
  324.6 8.2 shard_map.181
  356.5 8.0 shard_map.182
  392.7 10.2 %shard_map.183 = (bf16[144,768]{1,0:T(8,128)(2,1)}, bf16[528,768]{1,0:T(8,128)(2,1)}, bf16[528,768]{1,0:T(8,128)(2,1)}) custom-call(bf16[144,768]{1,0:T(8,128)(2,1)} %convolution_convert_fusion.24.q_ref, bf16[528,768]{1,0:T(8,128)(2,1)} %convolution_convert_fusion.13.k_ref, bf16[528,768]{1,0:T(8,128)(2,1)} %convolution_convert_fusion.12.v_ref, ...), custom_call_target="tpu_custom_call" | custom-call | flops 1167851520 | bytes 6000000 | tf_op jit(solution)/shard_map/pallas_call | solution.py:204
  411.3 7.7 collective-permute-done.50
  432.5 9.8 %shard_map.184 = (bf16[144,768]{1,0:T(8,128)(2,1)}, bf16[528,768]{1,0:T(8,128)(2,1)}, bf16[528,768]{1,0:T(8,128)(2,1)}) custom-call(bf16[144,768]{1,0:T(8,128)(2,1)} %convolution_convert_fusion.25.q_ref, bf16[528,768]{1,0:T(8,128)(2,1)} %convolution_convert_fusion.15.k_ref, bf16[528,768]{1,0:T(8,128)(2,1)} %convolution_convert_fusion.14.v_ref, ...), custom_call_target="tpu_custom_call" | custom-call | flops 1167851520 | bytes 6000000 | tf_op jit(solution)/shard_map/pallas_call | solution.py:204
  515.1 9.9 %shard_map.185 = (bf16[144,768]{1,0:T(8,128)(2,1)}, bf16[528,768]{1,0:T(8,128)(2,1)}, bf16[528,768]{1,0:T(8,128)(2,1)}) custom-call(bf16[144,768]{1,0:T(8,128)(2,1)} %convolution_convert_fusion.26.q_ref, bf16[528,768]{1,0:T(8,128)(2,1)} %convolution_convert_fusion.17.k_ref, bf16[528,768]{1,0:T(8,128)(2,1)} %convolution_convert_fusion.16.v_ref, ...), custom_call_target="tpu_custom_call" | custom-call | flops 1167851520 | bytes 6000000 | tf_op jit(solution)/shard_map/pallas_call | solution.py:204
  564.9 9.8 %shard_map.186 = (bf16[144,768]{1,0:T(8,128)(2,1)}, bf16[528,768]{1,0:T(8,128)(2,1)}, bf16[528,768]{1,0:T(8,128)(2,1)}) custom-call(bf16[144,768]{1,0:T(8,128)(2,1)} %convolution_convert_fusion.27.q_ref, bf16[528,768]{1,0:T(8,128)(2,1)} %convolution_convert_fusion.19.k_ref, bf16[528,768]{1,0:T(8,128)(2,1)} %convolution_convert_fusion.18.v_ref, ...), custom_call_target="tpu_custom_call" | custom-call | flops 1167851520 | bytes 6000000 | tf_op jit(solution)/shard_map/pallas_call | solution.py:204
  617.0 117.7 %all-reduce.4.cloned.1.call-done = f32[24,768]{1,0:T(8,128)} async-done(((f32[24,768]{1,0:T(8,128)}), f32[24,768]{1,0:T(8,128)}) %all-reduce.4.cloned.1.call-update) | async-done | bytes 73744 | tf_op jit(solution)/shard_map/psum | solution.py:501
  743.3 11.0 %collective-permute-done.77 = bf16[1,2,192,768]{3,2,1,0:T(8,128)(2,1)} collective-permute-done((bf16[1,2,192,768]{3,2,1,0:T(8,128)(2,1)}, bf16[1,2,192,768]{3,2,1,0:T(8,128)(2,1)}, u32[]{:S(2)}, u32[]{:S(2)}) %collective-permute-start.77) | collective-permute-done | bytes 589856 | tf_op jit(solution)/shard_map/ppermute | solution.py:17
  772.0 7.0 collective-permute-done.82
  804.2 23.2 %collective-permute-done.65 = bf16[1,1,192,768]{3,2,1,0:T(8,128)(2,1)S(1)} collective-permute-done((bf16[1,1,192,768]{3,2,1,0:T(8,128)(2,1)S(1)}, bf16[1,1,192,768]{3,2,1,0:T(8,128)(2,1)S(1)}, u32[]{:S(2)}, u32[]{:S(2)}) %collective-permute-start.65) | collective-permute-done | bytes 294944 | tf_op jit(solution)/shard_map/ppermute | solution.py:17
  837.2 10.9 %collective-permute-done.86 = bf16[1,1,192,1536]{3,2,1,0:T(8,128)(2,1)S(1)} collective-permute-done((bf16[1,1,192,1536]{3,2,1,0:T(8,128)(2,1)S(1)}, bf16[1,1,192,1536]{3,2,1,0:T(8,128)(2,1)S(1)}, u32[]{:S(2)}, u32[]{:S(2)}) %collective-permute-start.86) | collective-permute-done | bytes 589856 | tf_op jit(solution)/shard_map/ppermute | solution.py:17
  848.3 20.5 %collective-permute-done.89 = bf16[1,1,192,1536]{3,2,1,0:T(8,128)(2,1)S(1)} collective-permute-done((bf16[1,1,192,1536]{3,2,1,0:T(8,128)(2,1)S(1)}, bf16[1,1,192,1536]{3,2,1,0:T(8,128)(2,1)S(1)}, u32[]{:S(2)}, u32[]{:S(2)}) %collective-permute-start.89) | collective-permute-done | bytes 589856 | tf_op jit(solution)/shard_map/ppermute | solution.py:17
  873.6 8.8 collective-permute-done.70
  893.1 11.6 %collective-permute-done.74 = bf16[192,1536]{1,0:T(8,128)(2,1)S(1)} collective-permute-done((bf16[192,1536]{1,0:T(8,128)(2,1)S(1)}, bf16[192,1536]{1,0:T(8,128)(2,1)S(1)}, u32[]{:S(2)}, u32[]{:S(2)}) %collective-permute-start.74) | collective-permute-done | bytes 589856 | tf_op jit(solution)/shard_map/ppermute | solution.py:17
  906.5 9.8 %collective-permute-done.91 = bf16[192,768]{1,0:T(8,128)(2,1)S(1)} collective-permute-done((bf16[192,768]{1,0:T(8,128)(2,1)S(1)}, bf16[192,768]{1,0:T(8,128)(2,1)S(1)}, u32[]{:S(2)}, u32[]{:S(2)}) %collective-permute-start.91) | collective-permute-done | bytes 294944 | tf_op jit(solution)/shard_map/ppermute | solution.py:17
  (1256 shorter events, 498.0 us)
Async XLA Ops:
  7.2 727.4 %all-reduce.4.cloned.1.call-start = ((), (), s32[]{:S(2)}) async-start(), calls=%async_computation | async-start | bytes 147456 | tf_op jit(solution)/shard_map/psum | solution.py:501
  10.7 78.0 %collective-permute-start.1 = (bf16[192,1152]{1,0:T(8,128)(2,1)}, bf16[192,1152]{1,0:T(8,128)(2,1)}, u32[]{:S(2)}, u32[]{:S(2)}) collective-permute-start(bf16[192,1152]{1,0:T(8,128)(2,1)} %broadcast_select_fusion.15), channel_id=1, source_target_pairs={{0,1},{1,0},{2,3},{3,2},{4,5},{5,4},{6,7},{7,6},{8,9},{9,8},{10,11... | collective-permute-start | bytes 1327112 | tf_op jit(solution)/shard_map/ppermute | solution.py:17
  11.9 65.4 %collective-permute-start = (bf16[128,768]{1,0:T(8,128)(2,1)}, bf16[128,768]{1,0:T(8,128)(2,1)S(1)}, u32[]{:S(2)}, u32[]{:S(2)}) collective-permute-start(bf16[128,768]{1,0:T(8,128)(2,1)} %get-tuple-element.164), channel_id=1, source_target_pairs={{1,5},{3,7},{5,1},{7,3},{9,13},{11,15},{13,9},{15,11},{17,21},{19,... | collective-permute-start | bytes 589832 | tf_op jit(solution)/shard_map/ppermute | solution.py:28
  12.7 64.6 %collective-permute-start.41 = (bf16[128,768]{1,0:T(8,128)(2,1)S(1)}, bf16[128,768]{1,0:T(8,128)(2,1)S(1)}, u32[]{:S(2)}, u32[]{:S(2)}) collective-permute-start(bf16[128,768]{1,0:T(8,128)(2,1)S(1)} %get-tuple-element.163), channel_id=1, source_target_pairs={{1,5},{3,7},{5,1},{7,3},{9,13},{11,15},{13,9},{15,11},{17,21},{19,... | collective-permute-start | bytes 589832 | tf_op jit(solution)/shard_map/ppermute | solution.py:28
  14.2 68.9 %collective-permute-start.40 = (bf16[128,768]{1,0:T(8,128)(2,1)}, bf16[128,768]{1,0:T(8,128)(2,1)S(1)}, u32[]{:S(2)}, u32[]{:S(2)}) collective-permute-start(bf16[128,768]{1,0:T(8,128)(2,1)} %get-tuple-element.159), channel_id=1, source_target_pairs={{1,5},{3,7},{5,1},{7,3},{9,13},{11,15},{13,9},{15,11},{17,21},{19,... | collective-permute-start | bytes 589832 | tf_op jit(solution)/shard_map/ppermute | solution.py:28
  14.8 68.2 %collective-permute-start.48 = (bf16[128,768]{1,0:T(8,128)(2,1)}, bf16[128,768]{1,0:T(8,128)(2,1)}, u32[]{:S(2)}, u32[]{:S(2)}) collective-permute-start(bf16[128,768]{1,0:T(8,128)(2,1)} %get-tuple-element.160), channel_id=1, source_target_pairs={{1,5},{3,7},{5,1},{7,3},{9,13},{11,15},{13,9},{15,11},{17,21},{19,... | collective-permute-start | bytes 589832 | tf_op jit(solution)/shard_map/ppermute | solution.py:28
  90.2 42.0 %collective-permute-start.32 = (bf16[192,768]{1,0:T(8,128)(2,1)S(1)}, bf16[192,768]{1,0:T(8,128)(2,1)S(1)}, u32[]{:S(2)}, u32[]{:S(2)}) collective-permute-start(bf16[192,768]{1,0:T(8,128)(2,1)S(1)} %concatenate.568), channel_id=1, source_target_pairs={{0,4},{2,6},{4,0},{6,2},{1,5},{3,7},{5,1},{7,3},{8,12},{10,14},{12... | collective-permute-start | bytes 884744 | tf_op jit(solution)/shard_map/ppermute | solution.py:17
  90.2 44.2 %collective-permute-start.13 = (bf16[192,768]{1,0:T(8,128)(2,1)S(1)}, bf16[192,768]{1,0:T(8,128)(2,1)S(1)}, u32[]{:S(2)}, u32[]{:S(2)}) collective-permute-start(bf16[192,768]{1,0:T(8,128)(2,1)S(1)} %concatenate.566), channel_id=1, source_target_pairs={{0,4},{2,6},{4,0},{6,2},{1,5},{3,7},{5,1},{7,3},{8,12},{10,14},{12... | collective-permute-start | bytes 884744 | tf_op jit(solution)/shard_map/ppermute | solution.py:17
  93.2 38.7 %collective-permute-start.21 = (bf16[192,384]{1,0:T(8,128)(2,1)S(1)}, bf16[192,384]{1,0:T(8,128)(2,1)S(1)}, u32[]{:S(2)}, u32[]{:S(2)}) collective-permute-start(bf16[192,384]{1,0:T(8,128)(2,1)S(1)} %get-tuple-element.177), channel_id=1, source_target_pairs={{0,4},{2,6},{4,0},{6,2},{1,5},{3,7},{5,1},{7,3},{8,12},{10,14},{12... | collective-permute-start | bytes 442376 | tf_op jit(solution)/shard_map/ppermute | solution.py:17
  134.6 39.4 %collective-permute-start.14 = (bf16[192,1536]{1,0:T(8,128)(2,1)S(1)}, bf16[192,1536]{1,0:T(8,128)(2,1)S(1)}, u32[]{:S(2)}, u32[]{:S(2)}) collective-permute-start(bf16[192,1536]{1,0:T(8,128)(2,1)S(1)} %pad_maximum_fusion.16), channel_id=1, source_target_pairs={{0,2},{2,0},{4,6},{6,4},{1,3},{3,1},{5,7},{7,5},{8,10},{10,8},{12,... | collective-permute-start | bytes 1769480 | tf_op jit(solution)/shard_map/ppermute | solution.py:17
  209.1 38.3 %collective-permute-start.25 = (bf16[768,768]{1,0:T(8,128)(2,1)}, bf16[768,768]{1,0:T(8,128)(2,1)}, u32[]{:S(2)}, u32[]{:S(2)}) collective-permute-start(bf16[768,768]{1,0:T(8,128)(2,1)} %bitcast.28), channel_id=1, source_target_pairs={{0,1},{1,0},{2,3},{3,2},{4,5},{5,4},{6,7},{7,6},{8,9},{9,8},{10,11... | collective-permute-start | bytes 3538952 | tf_op jit(solution)/shard_map/ppermute | solution.py:17
  216.7 50.7 %collective-permute-start.37 = (bf16[2,1,192,1536]{3,2,1,0:T(8,128)(2,1)}, bf16[2,1,192,1536]{3,2,1,0:T(8,128)(2,1)}, u32[]{:S(2)}, u32[]{:S(2)}) collective-permute-start(bf16[2,1,192,1536]{3,2,1,0:T(8,128)(2,1)} %pad_maximum_fusion.11), channel_id=1, source_target_pairs={{0,8},{8,0},{16,24},{24,16},{1,9},{9,1},{17,25},{25,17},{2,10},{10... | collective-permute-start | bytes 3538952 | tf_op jit(solution)/shard_map/ppermute | solution.py:17
  270.3 42.6 %collective-permute-start.39 = (bf16[768,1536]{1,0:T(8,128)(2,1)}, bf16[768,1536]{1,0:T(8,128)(2,1)}, u32[]{:S(2)}, u32[]{:S(2)}) collective-permute-start(bf16[768,1536]{1,0:T(8,128)(2,1)} %bitcast.34), channel_id=1, source_target_pairs={{0,1},{1,0},{2,3},{3,2},{4,5},{5,4},{6,7},{7,6},{8,9},{9,8},{10,11... | collective-permute-start | bytes 7077896 | tf_op jit(solution)/shard_map/ppermute | solution.py:17
  467.4 270.1 %collective-permute-start.57 = (bf16[2,128,768]{2,1,0:T(8,128)(2,1)}, bf16[2,128,768]{2,1,0:T(8,128)(2,1)}, u32[]{:S(2)}, u32[]{:S(2)}) collective-permute-start(bf16[2,128,768]{2,1,0:T(8,128)(2,1)} %pad_maximum_fusion.33), channel_id=1, source_target_pairs={{0,1},{2,3},{4,5},{6,7},{8,9},{10,11},{12,13},{14,15},{16,17},{18,... | collective-permute-start | bytes 1179656 | tf_op jit(solution)/shard_map/ppermute | solution.py:28
  469.9 268.7 %collective-permute-start.59 = (bf16[2,128,768]{2,1,0:T(8,128)(2,1)}, bf16[2,128,768]{2,1,0:T(8,128)(2,1)}, u32[]{:S(2)}, u32[]{:S(2)}) collective-permute-start(bf16[2,128,768]{2,1,0:T(8,128)(2,1)} %pad_maximum_fusion.33), channel_id=1, source_target_pairs={{1,5},{3,7},{5,1},{7,3},{9,13},{11,15},{13,9},{15,11},{17,21},{19,... | collective-permute-start | bytes 1179656 | tf_op jit(solution)/shard_map/ppermute | solution.py:28
  537.9 64.4 %collective-permute-start.76 = (bf16[768,768]{1,0:T(8,128)(2,1)}, bf16[768,768]{1,0:T(8,128)(2,1)}, u32[]{:S(2)}, u32[]{:S(2)}) collective-permute-start(bf16[768,768]{1,0:T(8,128)(2,1)} %get-tuple-element.343), channel_id=1, source_target_pairs={{0,1},{1,0},{2,3},{3,2},{4,5},{5,4},{6,7},{7,6},{8,9},{9,8},{10,11... | collective-permute-start | bytes 3538952 | tf_op jit(solution)/shard_map/ppermute | solution.py:17
  540.3 58.9 %collective-permute-start.79 = (bf16[768,768]{1,0:T(8,128)(2,1)}, bf16[768,768]{1,0:T(8,128)(2,1)}, u32[]{:S(2)}, u32[]{:S(2)}) collective-permute-start(bf16[768,768]{1,0:T(8,128)(2,1)} %get-tuple-element.341), channel_id=1, source_target_pairs={{0,1},{1,0},{2,3},{3,2},{4,5},{5,4},{6,7},{7,6},{8,9},{9,8},{10,11... | collective-permute-start | bytes 3538952 | tf_op jit(solution)/shard_map/ppermute | solution.py:17
  597.8 182.4 %collective-permute-start.84 = (bf16[768,1536]{1,0:T(8,128)(2,1)}, bf16[768,1536]{1,0:T(8,128)(2,1)}, u32[]{:S(2)}, u32[]{:S(2)}) collective-permute-start(bf16[768,1536]{1,0:T(8,128)(2,1)} %convolution_convert_fusion.2), channel_id=1, source_target_pairs={{0,1},{1,0},{2,3},{3,2},{4,5},{5,4},{6,7},{7,6},{8,9},{9,8},{10,11... | collective-permute-start | bytes 7077896 | tf_op jit(solution)/shard_map/ppermute | solution.py:17
  599.2 185.4 %collective-permute-start.87 = (bf16[768,1536]{1,0:T(8,128)(2,1)}, bf16[768,1536]{1,0:T(8,128)(2,1)}, u32[]{:S(2)}, u32[]{:S(2)}) collective-permute-start(bf16[768,1536]{1,0:T(8,128)(2,1)} %convolution_convert_fusion), channel_id=1, source_target_pairs={{0,1},{1,0},{2,3},{3,2},{4,5},{5,4},{6,7},{7,6},{8,9},{9,8},{10,11... | collective-permute-start | bytes 7077896 | tf_op jit(solution)/shard_map/ppermute | solution.py:17
  615.5 124.6 %collective-permute-start.58 = (bf16[2,128,768]{2,1,0:T(8,128)(2,1)S(1)}, bf16[2,128,768]{2,1,0:T(8,128)(2,1)S(1)}, u32[]{:S(2)}, u32[]{:S(2)}) collective-permute-start(bf16[2,128,768]{2,1,0:T(8,128)(2,1)S(1)} %pad_maximum_fusion.32), channel_id=1, source_target_pairs={{1,4},{3,6},{5,0},{7,2},{9,12},{11,14},{13,8},{15,10},{17,20},{19,... | collective-permute-start | bytes 1179656 | tf_op jit(solution)/shard_map/ppermute | solution.py:28
  765.0 64.0 %collective-permute-start.68 = (bf16[768,1536]{1,0:T(8,128)(2,1)S(1)}, bf16[768,1536]{1,0:T(8,128)(2,1)S(1)}, u32[]{:S(2)}, u32[]{:S(2)}) collective-permute-start(bf16[768,1536]{1,0:T(8,128)(2,1)S(1)} %copy-done.274), channel_id=1, source_target_pairs={{0,1},{1,0},{2,3},{3,2},{4,5},{5,4},{6,7},{7,6},{8,9},{9,8},{10,11... | collective-permute-start | bytes 7077896 | tf_op jit(solution)/shard_map/ppermute | solution.py:17
  767.5 66.8 %collective-permute-start.71 = (bf16[768,1536]{1,0:T(8,128)(2,1)S(1)}, bf16[768,1536]{1,0:T(8,128)(2,1)S(1)}, u32[]{:S(2)}, u32[]{:S(2)}) collective-permute-start(bf16[768,1536]{1,0:T(8,128)(2,1)S(1)} %copy-done.273), channel_id=1, source_target_pairs={{0,1},{1,0},{2,3},{3,2},{4,5},{5,4},{6,7},{7,6},{8,9},{9,8},{10,11... | collective-permute-start | bytes 7077896 | tf_op jit(solution)/shard_map/ppermute | solution.py:17
  827.6 56.9 %collective-permute-start.66 = (bf16[192,768]{1,0:T(8,128)(2,1)S(1)}, bf16[192,768]{1,0:T(8,128)(2,1)S(1)}, u32[]{:S(2)}, u32[]{:S(2)}) collective-permute-start(bf16[192,768]{1,0:T(8,128)(2,1)S(1)} %pad_maximum_fusion.38), channel_id=1, source_target_pairs={{0,2},{2,0},{4,6},{6,4},{1,3},{3,1},{5,7},{7,5},{8,10},{10,8},{12,... | collective-permute-start | bytes 884744 | tf_op jit(solution)/shard_map/ppermute | solution.py:17
  830.6 38.4 %collective-permute-start.69 = (bf16[1,2,192,1536]{3,2,1,0:T(8,128)(2,1)S(1)}, bf16[1,2,192,1536]{3,2,1,0:T(8,128)(2,1)S(1)}, u32[]{:S(2)}, u32[]{:S(2)}) collective-permute-start(bf16[1,2,192,1536]{3,2,1,0:T(8,128)(2,1)S(1)} %bitcast.364), channel_id=1, source_target_pairs={{0,16},{8,24},{16,0},{24,8},{1,17},{9,25},{17,1},{25,9},{2,18},{10... | collective-permute-start | bytes 3538952 | tf_op jit(solution)/shard_map/ppermute | solution.py:17
  (358 other events, 3543.7 us)
Sparse Core Ops, SparseCore 0:
  615.5 119.0 all-reduce.3
